TPU v7x, 32 devices: a whole 2x2x4 slice. The times are simulated.
32 devices in a mesh: doc: 2 (over y), seq: 4 (over z), sub: 4 (over x, core).
Axes of the slice: x: 2, y: 2, z: 4, core: 2. Of those that a mesh axis runs over, the one named last changes fastest.
Arguments:
- queries: bfloat16 [16384, 512], P(('doc', 'seq', 'sub')), parts along dimension 0, may hold values from -18 to 18
- keys: bfloat16 [16384, 512], P(('doc', 'seq', 'sub')), parts along dimension 0, may hold values from -18 to 18
- values: bfloat16 [16384, 512], P(('doc', 'seq', 'sub')), parts along dimension 0, may hold values from -18 to 18
- seg_lengths: int32 [512], P('doc'), parts along dimension 0, may hold values from 1 to 64, 8192 in all
Outputs:
- attended: bfloat16 [16384, 512], P(('doc', 'seq', 'sub')), parts along dimension 0
There are 2 independent parts, one for each index of `doc`. A program takes and returns all parts, laid end to end along the dimension named above; each array names one. Nothing has to cross between parts.
Inputs may be any that keep to these rules, and one draw needn't show every extreme that they name: `seg_lengths`: the 256 segments cover all 8192 tokens in order; the longest has exactly 64 tokens.
All inputs are finite; a program needn't handle non-finite values.
Results may differ from a plain program's by a relative error of at most 0.012.
Values may be sent and summed in bfloat16 or wider, within the bound.
A program may use at most 64 MiB of HBM per device.

v0:
```python
import math

import jax
import jax.numpy as jnp
from jax import lax
from jax.sharding import PartitionSpec as P

H = 8
HD = 64
M = 256
ITERS = 3


HIGH_PRECISION = lax.Precision.HIGHEST


def row_softmax(score_matrix):
    row_top = jnp.max(score_matrix, axis=-1, keepdims=True)
    exponentials = jnp.exp(score_matrix - row_top)
    return exponentials / jnp.sum(exponentials, axis=-1, keepdims=True)


def iterative_pseudo_inverse(kernel):
    absval = jnp.abs(kernel)
    row_most = jnp.max(jnp.sum(absval, axis=2), axis=1)
    col_most = jnp.max(jnp.sum(absval, axis=1), axis=1)
    iterate = jnp.transpose(kernel, (0, 2, 1)) / (row_most * col_most)[:, None, None]
    identity = jnp.eye(kernel.shape[1], dtype=jnp.float32)[None]
    for sweep in range(ITERS):
        product = jnp.einsum("hij,hjk->hik", kernel, iterate, precision=HIGH_PRECISION)
        nested = jnp.einsum(
            "hij,hjk->hik", product, 7.0 * identity - product, precision=HIGH_PRECISION
        )
        nested = jnp.einsum(
            "hij,hjk->hik", product, 15.0 * identity - nested, precision=HIGH_PRECISION
        )
        iterate = 0.25 * jnp.einsum(
            "hij,hjk->hik", iterate, 13.0 * identity - nested, precision=HIGH_PRECISION
        )
    return iterate


def solve_mixing(query_head_rows, key_head_rows, landmark_values, score_scaling):
    landmark_kernel = row_softmax(
        jnp.einsum(
            "raj,taj->art", query_head_rows, key_head_rows, preferred_element_type=jnp.float32
        )
        * score_scaling
    )
    approx_inverse = iterative_pseudo_inverse(landmark_kernel)
    return jnp.einsum(
        "gux,gxr->gur", approx_inverse, landmark_values, precision=HIGH_PRECISION
    ).astype(jnp.bfloat16)


def shards(queries, keys, values, seg_lengths):
    row_count = queries.shape[0]
    width = queries.shape[1]
    score_scaling = 1.0 / math.sqrt(HD)
    shard = lax.axis_index("seq") * lax.axis_size("sub") + lax.axis_index("sub")
    positions = shard * row_count + lax.iota(jnp.int32, row_count)
    seg_ends = jnp.cumsum(seg_lengths)
    seg_begins = seg_ends - seg_lengths
    member = (
        (positions[:, None] >= seg_begins[None, :]) & (positions[:, None] < seg_ends[None, :])
    ).astype(jnp.bfloat16)
    counts = seg_lengths.astype(jnp.float32)
    contract = (((0,), (0,)), ((), ()))
    q_part = lax.dot_general(member, queries, contract, preferred_element_type=jnp.float32)
    k_part = lax.dot_general(member, keys, contract, preferred_element_type=jnp.float32)
    q_sums, k_sums = lax.psum((q_part, k_part), ("seq", "sub"))
    query_landmarks = (q_sums / counts[:, None]).astype(jnp.bfloat16)
    key_landmarks = (k_sums / counts[:, None]).astype(jnp.bfloat16)
    query_head_rows = query_landmarks.reshape(M, H, HD)
    key_head_rows = key_landmarks.reshape(M, H, HD)
    value_head_rows = values.reshape(row_count, H, HD)
    score_matrix = (
        jnp.einsum(
            "czy,rzy->zcr",
            query_head_rows,
            keys.reshape(row_count, H, HD),
            preferred_element_type=jnp.float32,
        )
        * score_scaling
    )
    row_top = lax.pmax(jnp.max(score_matrix, axis=2), ("seq", "sub"))
    exponentials = jnp.exp(score_matrix - row_top[:, :, None])
    total = jnp.sum(exponentials, axis=2)
    numer = jnp.einsum(
        "ijv,vib->ijb",
        exponentials,
        value_head_rows,
        precision=HIGH_PRECISION,
        preferred_element_type=jnp.float32,
    )
    total, numer = lax.psum((total, numer), ("seq", "sub"))
    landmark_values = numer / total[:, :, None]
    mixing_matrix = solve_mixing(query_head_rows, key_head_rows, landmark_values, score_scaling)
    scores_one = (
        jnp.einsum(
            "fxp,oxp->fxo",
            queries.reshape(row_count, H, HD),
            key_head_rows,
            preferred_element_type=jnp.float32,
        )
        * score_scaling
    )
    weight_matrix = row_softmax(scores_one).astype(jnp.bfloat16)
    attended = jnp.einsum(
        "ugf,gfa->uga", weight_matrix, mixing_matrix, preferred_element_type=jnp.float32
    )
    return attended.reshape(row_count, width).astype(jnp.bfloat16)


def solution(mesh):
    placed = (
        P(("doc", "seq", "sub"), None),
        P(("doc", "seq", "sub"), None),
        P(("doc", "seq", "sub"), None),
        P("doc"),
    )
    return jax.shard_map(
        shards,
        mesh=mesh,
        in_specs=placed,
        out_specs=P(("doc", "seq", "sub"), None),
        check_vma=False,
    )
```

profile of v0, /device:TPU:1, one launch (start us, length us, event | category | flops | bytes accessed | tf_op | source)
XLA Modules:
  0.0 318.4 jit_solution(4167720343065813831)
XLA Ops:
  6.5 1.1 reduce-window.9
  7.6 0.1 slice.7
  7.8 0.1 slice_reduce_fusion
  7.9 0.8 fusion.74
  8.7 2.3 fusion.59
  11.0 0.0 all-reduce.4.cloned.1.call-update
  11.0 0.0 all-reduce.6.cloned.1.call-start
  11.1 0.0 copy-done.6
  11.1 1.1 copy.33
  12.2 0.2 copy.32
  12.4 0.2 copy.31
  12.6 1.2 fusion.58
  13.8 90.1 %all-reduce.4.cloned.1.call-done = f32[256,512]{1,0:T(8,128)} async-done(((f32[256,512]{1,0:T(8,128)}), f32[256,512]{1,0:T(8,128)}) %all-reduce.4.cloned.1.call-update) | async-done | bytes 524304 | tf_op jit(solution)/shard_map/psum | solution.py:71
  104.0 1.1 divide_convert_fusion.5
  105.1 0.1 copy.26
  105.3 2.7 multiply_reduce_fusion
  107.9 29.3 %pmax.7 = f32[8,256]{1,0:T(8,128)S(1)} all-reduce(f32[8,256]{1,0:T(8,128)S(1)} %get-tuple-element.12), channel_id=1, replica_groups=mesh['doc'=2,'seq'=4,'sub'=4] {'seq','sub'}, use_global_device_ids=true, to_apply=%region_11.12 | all-reduce | flops 2048 | bytes 16384 | tf_op jit(solution)/shard_map/pmax | solution.py:86
  137.3 5.8 %fusion.6 = f32[8,256,64]{1,2,0:T(8,128)} fusion(bf16[512,8,64]{0,2,1:T(8,128)(2,1)S(1)} %bitcast.54, f32[8,256,512]{2,1,0:T(8,128)} %get-tuple-element.13, f32[8,256]{1,0:T(8,128)S(1)} %pmax.7), kind=kOutput, calls=%fused_computation.11 | convolution fusion | flops 807403520 | bytes 5251072 | tf_op jit(solution)/shard_map/ijv,vib->ijb/dot_general | solution.py:89
  143.1 0.0 all-reduce.6.cloned.1.call-update
  143.2 3.1 fusion.5
  146.3 32.9 %psum.31 = f32[8,256]{1,0:T(8,128)S(1)} all-reduce(f32[8,256]{1,0:T(8,128)S(1)} %fusion.5), channel_id=1, replica_groups=mesh['doc'=2,'seq'=4,'sub'=4] {'seq','sub'}, use_global_device_ids=true, to_apply=%region_14.15 | all-reduce | flops 2048 | bytes 16384 | tf_op jit(solution)/shard_map/psum | solution.py:96
  179.2 56.7 %all-reduce.6.cloned.1.call-done = (f32[256,512]{1,0:T(8,128)}, f32[8,256,64]{1,2,0:T(8,128)}) async-done(((f32[256,512]{1,0:T(8,128)}, f32[8,256,64]{1,2,0:T(8,128)}), (f32[256,512]{1,0:T(8,128)}, f32[8,256,64]{1,2,0:T(8,128)})) %all-reduce.6.cloned.1.call-update) | async-done | bytes 1048592 | tf_op jit(solution)/shard_map/psum | solution.py:71
  235.9 1.1 divide_convert_fusion.4
  237.0 0.1 copy.27
  237.2 1.8 convolution_multiply_fusion
  239.0 1.0 fusion.75
  240.0 0.7 fusion.53
  240.7 0.1 reduce_max.47
  240.8 0.1 reduce_max.46
  240.9 1.7 bitcast_divide_fusion
  242.6 2.9 copy.29
  245.5 8.1 %online-softmax = f32[8,256,256]{2,1,0:T(8,128)} custom-call(f32[8,256,256]{2,1,0:T(8,128)} %convolution_multiply_fusion, f32[8,256,256]{2,1,0:T(8,128)} %copy.29), custom_call_target="tpu_custom_call" | custom-call | tf_op online-softmax
  253.6 4.6 %fusion.13 = f32[8,256,256]{2,1,0:T(8,128)S(1)} fusion(f32[8,256,256]{2,1,0:T(8,128)} %online-softmax, f32[256,256]{1,0:T(8,128)S(1)} %fusion.61), kind=kOutput, calls=%fused_computation.16 | convolution fusion | flops 1611137024 | bytes 4456448 | tf_op jit(solution)/shard_map/hij,hjk->hik/dot_general | solution.py:31
  258.2 2.3 fusion.30
  260.5 0.0 copy-done.5
  260.5 5.0 %fusion.33 = f32[8,256,256]{2,1,0:T(8,128)} fusion(f32[8,256,256]{1,2,0:T(8,128)S(1)} %copy-done.5, f32[8,256,256]{2,1,0:T(8,128)S(1)} %fusion.30, f32[256,256]{1,0:T(8,128)S(1)} %fusion.63), kind=kOutput, calls=%fused_computation.39 | convolution fusion | flops 1611661312 | bytes 6553600 | tf_op jit(solution)/shard_map/hij,hjk->hik/dot_general | solution.py:37
  265.5 8.1 %online-softmax.1 = f32[8,256,256]{2,1,0:T(8,128)} custom-call(f32[8,256,256]{2,1,0:T(8,128)} %convolution_multiply_fusion, f32[8,256,256]{2,1,0:T(8,128)} %fusion.33), custom_call_target="tpu_custom_call" | custom-call | tf_op online-softmax
  273.6 4.6 %fusion.11 = f32[8,256,256]{2,1,0:T(8,128)S(1)} fusion(f32[8,256,256]{2,1,0:T(8,128)} %online-softmax.1, f32[256,256]{1,0:T(8,128)S(1)} %fusion.61), kind=kOutput, calls=%fused_computation.14 | convolution fusion | flops 1611137024 | bytes 4456448 | tf_op jit(solution)/shard_map/hij,hjk->hik/dot_general | solution.py:31
  278.2 2.3 fusion.26
  280.4 3.5 %fusion.36 = f32[8,256,256]{2,1,0:T(8,128)} fusion(f32[8,256,256]{2,1,0:T(8,128)S(1)} %copy-done.4, f32[8,256,256]{2,1,0:T(8,128)S(1)} %fusion.26, f32[256,256]{1,0:T(8,128)S(1)} %fusion.63), kind=kOutput, calls=%fused_computation.40 | convolution fusion | flops 1611661312 | bytes 6553600 | tf_op jit(solution)/shard_map/hij,hjk->hik/dot_general | solution.py:37
  284.0 8.1 %online-softmax.2 = f32[8,256,256]{2,1,0:T(8,128)} custom-call(f32[8,256,256]{2,1,0:T(8,128)} %convolution_multiply_fusion, f32[8,256,256]{2,1,0:T(8,128)} %fusion.36), custom_call_target="tpu_custom_call" | custom-call | tf_op online-softmax
  292.1 4.6 %fusion.9 = f32[8,256,256]{2,1,0:T(8,128)S(1)} fusion(f32[8,256,256]{2,1,0:T(8,128)} %online-softmax.2, f32[256,256]{1,0:T(8,128)S(1)} %fusion.61), kind=kOutput, calls=%fused_computation.12 | convolution fusion | flops 1611137024 | bytes 4456448 | tf_op jit(solution)/shard_map/hij,hjk->hik/dot_general | solution.py:31
  296.7 2.3 fusion.22
  299.0 2.2 fusion.20
  301.2 3.4 %fusion.76 = (f32[512,8]{0,1:T(8,128)S(1)}, f32[512,8,256]{0,2,1:T(8,128)}) fusion(bf16[256,8,64]{0,2,1:T(8,128)(2,1)S(1)} %bitcast.53, bf16[512,8,64]{0,2,1:T(8,128)(2,1)S(1)} %bitcast.56), kind=kOutput, calls=%fused_computation.83 | convolution fusion | flops 137363712 | bytes 4997120 | tf_op jit(solution)/shard_map/sub | solution.py:19
  304.6 3.2 %fusion.40 = bf16[8,256,64]{1,2,0:T(8,128)(2,1)S(1)} fusion(f32[8,256,256]{2,1,0:T(8,128)S(1)} %fusion.20, f32[8,256,64]{1,2,0:T(8,128)} %get-tuple-element.8, f32[8,256]{1,0:T(8,128)S(1)} %psum.31), kind=kOutput, calls=%fused_computation.43 | convolution fusion | flops 403439616 | bytes 2891776 | tf_op jit(solution)/shard_map/gux,gxr->gur/dot_general | solution.py:51
  307.8 2.7 fusion.39
  310.5 1.0 copy.35
  (25 shorter events, 0.1 us)
Async XLA Ops:
  6.5 4.5 %copy-start.6 = (bf16[512,512]{1,0:T(8,128)(2,1)S(1)}, bf16[512,512]{1,0:T(8,128)(2,1)}, u32[]{:S(2)}) copy-start(bf16[512,512]{1,0:T(8,128)(2,1)} %param.4) | copy-start | bytes 1572868
  6.5 5.6 %copy-start.8 = (bf16[512,512]{1,0:T(8,128)(2,1)S(1)}, bf16[512,512]{1,0:T(8,128)(2,1)}, u32[]{:S(2)}) copy-start(bf16[512,512]{1,0:T(8,128)(2,1)} %param.6) | copy-start | bytes 1572868
  6.5 5.8 %copy-start.7 = (bf16[512,512]{1,0:T(8,128)(2,1)S(1)}, bf16[512,512]{1,0:T(8,128)(2,1)}, u32[]{:S(2)}) copy-start(bf16[512,512]{1,0:T(8,128)(2,1)} %param.5) | copy-start | bytes 1572868
  6.5 97.4 %all-reduce.4.cloned.1.call-start = ((), (), s32[]{:S(2)}) async-start(), calls=%async_computation | async-start | bytes 1048576 | tf_op jit(solution)/shard_map/psum | solution.py:71
  11.0 224.9 %all-reduce.6.cloned.1.call-start = ((), (), s32[]{:S(2)}) async-start(), calls=%async_computation.1 | async-start | bytes 2097152 | tf_op jit(solution)/shard_map/psum | solution.py:71
  253.6 4.6 %copy-start.1 = (f32[8,256,256]{2,1,0:T(8,128)S(1)}, f32[8,256,256]{2,1,0:T(8,128)}, u32[]{:S(2)}) copy-start(f32[8,256,256]{2,1,0:T(8,128)} %online-softmax) | copy-start | bytes 6291460
  258.2 2.3 copy-start.5
  273.6 4.6 %copy-start.2 = (f32[8,256,256]{2,1,0:T(8,128)S(1)}, f32[8,256,256]{2,1,0:T(8,128)}, u32[]{:S(2)}) copy-start(f32[8,256,256]{2,1,0:T(8,128)} %online-softmax.1) | copy-start | bytes 6291460
  278.1 2.3 copy-start.4
  292.1 4.6 %copy-start = (f32[8,256,256]{2,1,0:T(8,128)S(1)}, f32[8,256,256]{2,1,0:T(8,128)}, u32[]{:S(2)}) copy-start(f32[8,256,256]{2,1,0:T(8,128)} %online-softmax.2) | copy-start | bytes 6291460
  296.7 2.3 copy-start.3
  298.9 2.2 copy-start.9
Sparse Core Ops, SparseCore 0:
  11.1 92.7 all-reduce.3
  143.2 92.5 all-reduce.5
where the time goes:
time: 321 us; the launch traced here: 318 us
  waiting for transfers between devices  147 us (46%)
  blocking collectives  62.2 us (19%)
  matrix products  55.3 us (17%)
  Pallas kernels  24.3 us (8%)
  between operations  13.7 us (4%)
  other arithmetic  10 us (3%)
  local copies, waits for them, and re-layouts  5.91 us (2%)
    psum x2, waiting for transfers between devices, shards(): q_sums, k_sums = lax.psum((q_part, k_part), ('seq', 'sub'))  147 us
    psum x1, blocking collectives, shards(): total, numer = lax.psum((total, numer), ('seq', 'sub'))  32.9 us
    pmax x1, blocking collectives, shards(): row_top = lax.pmax(jnp.max(score_matrix, axis=2), ('seq', 'sub'))  29.3 us
    unnamed x3, Pallas kernels  24.3 us
    dot_general x3, matrix products, iterative_pseudo_inverse(): jnp.einsum('hij,hjk->hik', product, 7.0 * identity - product, precision=H...  13.7 us
    dot_general x3, matrix products, iterative_pseudo_inverse(): jnp.einsum('hij,hjk->hik', iterate, 13.0 * identity - nested, precision=H...  10.7 us
    dot_general x3, matrix products, iterative_pseudo_inverse(): jnp.einsum('hij,hjk->hik', product, 15.0 * identity - nested, precision=H...  6.81 us
  transfers between devices with their start and end apart: 2, of which 2 were waited for; matrix products, arithmetic and copies ran while one was open for 2% of the time, Pallas kernels for 0%

commit v1 on v0

--- a/solution.py
+++ b/solution.py
@@ -1,8 +1,11 @@
+import functools
 import math
 
 import jax
 import jax.numpy as jnp
 from jax import lax
+from jax.experimental import pallas as pl
+from jax.experimental.pallas import tpu as pltpu
 from jax.sharding import PartitionSpec as P
 
 H = 8
@@ -15,9 +18,9 @@
 
 
 def row_softmax(score_matrix):
-    row_top = jnp.max(score_matrix, axis=-1, keepdims=True)
+    row_top = lax.optimization_barrier(jnp.max(score_matrix, axis=-1, keepdims=True))
     exponentials = jnp.exp(score_matrix - row_top)
-    return exponentials / jnp.sum(exponentials, axis=-1, keepdims=True)
+    return exponentials / lax.optimization_barrier(jnp.sum(exponentials, axis=-1, keepdims=True))
 
 
 def iterative_pseudo_inverse(kernel):
@@ -59,7 +62,8 @@
     score_scaling = 1.0 / math.sqrt(HD)
     shard = lax.axis_index("seq") * lax.axis_size("sub") + lax.axis_index("sub")
     positions = shard * row_count + lax.iota(jnp.int32, row_count)
-    seg_ends = jnp.cumsum(seg_lengths)
+    earlier = lax.broadcasted_iota(jnp.int32, (M, M), 0) <= lax.broadcasted_iota(jnp.int32, (M, M), 1)
+    seg_ends = jnp.sum(jnp.where(earlier, seg_lengths[:, None], 0), axis=0)
     seg_begins = seg_ends - seg_lengths
     member = (
         (positions[:, None] >= seg_begins[None, :]) & (positions[:, None] < seg_ends[None, :])
@@ -112,6 +116,273 @@
     return attended.reshape(row_count, width).astype(jnp.bfloat16)
 
 
+F32 = jnp.float32
+BF16 = jnp.bfloat16
+TN = (((0,), (0,)), ((), ()))
+NN = (((1,), (0,)), ((), ()))
+NT = (((1,), (1,)), ((), ()))
+
+
+def dot(a, b, dims=NN):
+    return lax.dot_general(a, b, dims, preferred_element_type=F32)
+
+
+def split(a):
+    high = a.astype(BF16)
+    return high, (a - high.astype(F32)).astype(BF16)
+
+
+def dot3(a, b, dims=NN):
+    a_high, a_low = split(a)
+    b_high, b_low = split(b)
+    return dot(a_high, b_high, dims) + (dot(a_high, b_low, dims) + dot(a_low, b_high, dims))
+
+
+def fused(
+    n_seq,
+    n_sub,
+    q_ref,
+    k_ref,
+    v_ref,
+    len_ref,
+    out_ref,
+    part,
+    part_in,
+    land,
+    numer,
+    numer_in,
+    stats,
+    stats_in,
+    mix,
+    weights,
+    send_sem,
+    recv_sem,
+):
+    n = n_seq * n_sub
+    rows, width = q_ref.shape
+    block = width // n
+    per = HD // block
+    pairs = H // 2
+    scaling = 1.0 / math.sqrt(HD)
+    me = lax.axis_index("seq") * n_sub + lax.axis_index("sub")
+
+    def place(p):
+        return {"seq": lax.div(p, n_sub), "sub": lax.rem(p, n_sub)}
+
+    def peer(step):
+        return lax.rem(me + step, n)
+
+    def remote(phase, p, source, target):
+        return pltpu.make_async_remote_copy(
+            src_ref=source,
+            dst_ref=target,
+            send_sem=send_sem.at[phase, p],
+            recv_sem=recv_sem.at[phase, me],
+            device_id=place(p),
+            device_id_type=pl.DeviceIdType.MESH,
+        )
+
+    def arrival(phase, p, target):
+        pltpu.make_async_remote_copy(
+            src_ref=target,
+            dst_ref=target,
+            send_sem=send_sem.at[phase, p],
+            recv_sem=recv_sem.at[phase, p],
+            device_id=place(p),
+            device_id_type=pl.DeviceIdType.MESH,
+        ).wait_recv()
+
+    def each_peer(act):
+        def body(step, carry):
+            act(peer(step))
+            return carry
+
+        lax.fori_loop(1, n, body, 0)
+
+    barrier = pltpu.get_barrier_semaphore()
+    each_peer(
+        lambda p: pl.semaphore_signal(
+            barrier, inc=1, device_id=place(p), device_id_type=pl.DeviceIdType.MESH
+        )
+    )
+
+    lengths = len_ref[...].astype(F32)
+    upto = (
+        lax.broadcasted_iota(jnp.int32, (M, M), 0) <= lax.broadcasted_iota(jnp.int32, (M, M), 1)
+    ).astype(F32)
+    ends = lax.dot_general(
+        jnp.broadcast_to(lengths, (8, M)),
+        upto,
+        NN,
+        precision=HIGH_PRECISION,
+        preferred_element_type=F32,
+    )[0:1]
+    begins = ends - lengths
+    positions = (me * rows + lax.broadcasted_iota(jnp.int32, (rows, M), 0)).astype(F32)
+    member = ((positions >= begins) & (positions < ends)).astype(F32).astype(BF16)
+    inverse_lengths = 1.0 / lengths
+    for which, ref in enumerate((q_ref, k_ref)):
+        means = (dot(ref[...], member, TN) * inverse_lengths).astype(BF16)
+        for p in range(n):
+            part[p, which * block : (which + 1) * block, :] = means[p * block : (p + 1) * block]
+
+    pl.semaphore_wait(barrier, n - 1)
+    each_peer(lambda p: remote(0, p, part.at[p], part_in.at[me]).start())
+
+    def add_part(step, total):
+        p = peer(step)
+        arrival(0, p, part_in.at[p])
+        return total + part_in[p].astype(F32)
+
+    total = lax.fori_loop(1, n, add_part, part[me].astype(F32))
+    land[me] = total.astype(BF16)
+    each_peer(lambda p: remote(1, p, land.at[me], land.at[me]).start())
+
+    first = lax.div(me, per) * per
+    for i in range(per):
+        p = first + i
+
+        @pl.when(p != me)
+        def _():
+            arrival(1, p, land.at[p])
+
+    q_head = jnp.concatenate([land[first + i, :block] for i in range(per)], axis=0)
+    k_head = jnp.concatenate([land[first + i, block:] for i in range(per)], axis=0)
+    scores = dot(q_head, k_head, TN) * scaling
+    exponentials = jnp.exp(scores - jnp.max(scores, axis=1, keepdims=True))
+    kernel_two = exponentials / jnp.sum(exponentials, axis=1, keepdims=True)
+    absval = jnp.abs(kernel_two)
+    row_most = jnp.max(jnp.sum(absval, axis=1, keepdims=True), axis=0, keepdims=True)
+    col_most = jnp.max(jnp.sum(absval, axis=0, keepdims=True), axis=1, keepdims=True)
+    inverse = kernel_two.T / (row_most * col_most)
+    identity = (
+        lax.broadcasted_iota(jnp.int32, (M, M), 0) == lax.broadcasted_iota(jnp.int32, (M, M), 1)
+    ).astype(F32)
+    for sweep in range(ITERS):
+        product = dot3(kernel_two, inverse)
+        nested = dot3(product, 7.0 * identity - product)
+        nested = dot3(product, 15.0 * identity - nested)
+        inverse = 0.25 * dot3(inverse, 13.0 * identity - nested)
+
+    def other_arrival(p):
+        @pl.when(lax.div(p, per) != lax.div(me, per))
+        def _():
+            arrival(1, p, land.at[p])
+
+    each_peer(other_arrival)
+
+    row = lax.broadcasted_iota(jnp.int32, (2 * HD, M), 0)
+
+    def pair_operand(g, offset):
+        both = jnp.concatenate(
+            [land[p, offset : offset + block] for p in range(2 * g * per, 2 * (g + 1) * per)],
+            axis=0,
+        )
+        zero = jnp.zeros_like(both)
+        return jnp.concatenate(
+            [jnp.where(row < HD, both, zero), jnp.where(row < HD, zero, both)], axis=1
+        )
+
+    stats[...] = jnp.zeros_like(stats)
+    for g in range(pairs):
+        lanes = slice(g * 2 * HD, (g + 1) * 2 * HD)
+        scores = dot(k_ref[:, lanes], pair_operand(g, 0)) * scaling
+        top = jnp.max(scores, axis=0, keepdims=True)
+        exponentials = jnp.exp(scores - top)
+        sums = jnp.sum(exponentials, axis=0, keepdims=True)
+        both = dot(v_ref[:, lanes], exponentials.astype(BF16), TN)
+        for side in range(2):
+            head = 2 * g + side
+            columns = slice(side * M, (side + 1) * M)
+            stats[head, 0:1, :] = top[:, columns]
+            stats[head, 1:2, :] = sums[:, columns]
+            for i in range(per):
+                begin = side * HD + i * block
+                numer[head * per + i] = both[begin : begin + block, columns].astype(BF16)
+
+    def send_numer(p):
+        remote(2, p, numer.at[p], numer_in.at[me]).start()
+        remote(3, p, stats.at[lax.div(p, per)], stats_in.at[me]).start()
+
+    each_peer(send_numer)
+    numer_in[me] = numer[me]
+    stats_in[me] = stats[lax.div(me, per)]
+
+    for g in range(pairs):
+        lanes = slice(g * 2 * HD, (g + 1) * 2 * HD)
+        scores = dot(q_ref[:, lanes], pair_operand(g, block)) * scaling
+        for side in range(2):
+            mine = scores[:, side * M : (side + 1) * M]
+            weights[2 * g + side] = jnp.exp(mine - jnp.max(mine, axis=1, keepdims=True)).astype(BF16)
+
+    def numer_arrival(p):
+        arrival(2, p, numer_in.at[p])
+        arrival(3, p, stats_in.at[p])
+
+    each_peer(numer_arrival)
+    tops = [stats_in[p, 0:1, :] for p in range(n)]
+    top = functools.reduce(jnp.maximum, tops)
+    total = jnp.zeros((1, M), F32)
+    land_values = jnp.zeros((block, M), F32)
+    for p in range(n):
+        factor = jnp.exp(tops[p] - top)
+        total += factor * stats_in[p, 1:2, :]
+        land_values += factor * numer_in[p].astype(F32)
+    mix[me] = dot3(land_values / total, inverse, NT).astype(BF16)
+    each_peer(lambda p: remote(4, p, mix.at[me], mix.at[me]).start())
+    each_peer(lambda p: arrival(4, p, mix.at[p]))
+
+    ones = jnp.ones((HD, M), BF16)
+    low = lax.broadcasted_iota(jnp.int32, (rows, 2 * HD), 1) < HD
+    for g in range(pairs):
+        mixed = [
+            jnp.concatenate([mix[(2 * g + side) * per + i] for i in range(per)], axis=0)
+            for side in range(2)
+        ]
+        left = dot(weights[2 * g], jnp.concatenate([mixed[0], ones], axis=0), NT)
+        right = dot(weights[2 * g + 1], jnp.concatenate([ones, mixed[1]], axis=0), NT)
+        sums = pltpu.roll(jnp.where(low, right, left), HD, 1)
+        out_ref[:, g * 2 * HD : (g + 1) * 2 * HD] = (jnp.where(low, left, right) / sums).astype(BF16)
+
+    def drain(p):
+        remote(0, p, part.at[p], part_in.at[me]).wait_send()
+        remote(1, p, land.at[me], land.at[me]).wait_send()
+        remote(2, p, numer.at[p], numer_in.at[me]).wait_send()
+        remote(3, p, stats.at[lax.div(p, per)], stats_in.at[me]).wait_send()
+        remote(4, p, mix.at[me], mix.at[me]).wait_send()
+
+    each_peer(drain)
+
+
+def fused_shards(n_seq, n_sub, queries, keys, values, seg_lengths):
+    n = n_seq * n_sub
+    rows, width = queries.shape
+    block = width // n
+    vmem = pl.BlockSpec(memory_space=pltpu.VMEM)
+    return pl.pallas_call(
+        functools.partial(fused, n_seq, n_sub),
+        out_shape=jax.ShapeDtypeStruct((rows, width), BF16),
+        in_specs=[vmem] * 4,
+        out_specs=vmem,
+        scratch_shapes=[
+            pltpu.VMEM((n, 2 * block, M), BF16),
+            pltpu.VMEM((n, 2 * block, M), BF16),
+            pltpu.VMEM((n, 2 * block, M), BF16),
+            pltpu.VMEM((n, block, M), BF16),
+            pltpu.VMEM((n, block, M), BF16),
+            pltpu.VMEM((H, 8, M), F32),
+            pltpu.VMEM((n, 8, M), F32),
+            pltpu.VMEM((n, block, M), BF16),
+            pltpu.VMEM((H, rows, M), BF16),
+            pltpu.SemaphoreType.DMA((5, n)),
+            pltpu.SemaphoreType.DMA((5, n)),
+        ],
+        compiler_params=pltpu.CompilerParams(
+            collective_id=0, has_side_effects=True, vmem_limit_bytes=48 * 2**20
+        ),
+    )(queries, keys, values, seg_lengths.reshape(1, M))
+
+
 def solution(mesh):
     placed = (
         P(("doc", "seq", "sub"), None),
@@ -119,8 +390,11 @@
         P(("doc", "seq", "sub"), None),
         P("doc"),
     )
+    n_seq, n_sub = mesh.shape["seq"], mesh.shape["sub"]
+    block = H * HD // (n_seq * n_sub)
+    whole_tiles = block % 16 == 0 and HD % block == 0 and block * n_seq * n_sub == H * HD
     return jax.shard_map(
-        shards,
+        functools.partial(fused_shards, n_seq, n_sub) if whole_tiles else shards,
         mesh=mesh,
         in_specs=placed,
         out_specs=P(("doc", "seq", "sub"), None),

time: 321 us -> 56.7 us (0.18)
  waiting for transfers between devices: 147 us -> 0 us
  blocking collectives: 62.2 us -> 0 us
  matrix products: 55.3 us -> 0 us
  Pallas kernels: 24.3 us -> 51.5 us
  between operations: 13.7 us -> 0.01 us
  other arithmetic: 10 us -> 0 us
    psum x2 -> x0, waiting for transfers between devices: 147 us -> none  [shards(): q_sums, k_sums = lax.psum((q_part, k_part), ('seq', 'sub'))]
    pallas_call x0 -> x1, Pallas kernels: none -> 51.5 us  [fused_shards(): pl.pallas_call(functools.partial(fused, n_seq, n_sub), out_shape=jax.Shap...]
    dot_general x16 -> x0, matrix products: 51 us -> none  [the longest x3 13.7 us: iterative_pseudo_inverse(): jnp.einsum('hij,hjk->hik', product, 7.0 * identity - product, precision=H...]
    psum x1 -> x0, blocking collectives: 32.9 us -> none  [shards(): total, numer = lax.psum((total, numer), ('seq', 'sub'))]
    pmax x1 -> x0, blocking collectives: 29.3 us -> none  [shards(): row_top = lax.pmax(jnp.max(score_matrix, axis=2), ('seq', 'sub'))]
    unnamed x3 -> x0, Pallas kernels: 24.3 us -> none
    sub x2 -> x0, matrix products: 4.37 us -> none  [row_softmax(): exponentials = jnp.exp(score_matrix - row_top)]
    reduce_sum x2 -> x0, other arithmetic: 3.81 us -> none  [the longest x1 3.14 us: shards(): total = jnp.sum(exponentials, axis=2)]
  transfers between devices with their start and end apart: 2 -> 0, of which waited for: 2 -> 0; matrix products, arithmetic and copies ran while one was open for 2% -> 0% of each run, Pallas kernels for 0% -> 0%
where the time goes in v1:
time: 56.7 us; the launch traced here: 56.1 us
  Pallas kernels  51.5 us (91%)
  local copies, waits for them, and re-layouts  4.6 us (8%)
    pallas_call x1, Pallas kernels, fused_shards(): pl.pallas_call(functools.partial(fused, n_seq, n_sub), out_shape=jax.Shap...  51.5 us
    unnamed x9, local copies, waits for them, and re-layouts  4.6 us

profile of v1, /device:TPU:1, one launch (start us, length us, event | category | flops | bytes accessed | tf_op | source)
XLA Modules:
  0.0 56.1 jit_solution(15227514470705040322)
XLA Ops:
  0.0 0.0 copy-start.3
  0.0 0.7 %copy-done.3 = s32[256]{0:T(256)S(1)} copy-done((s32[256]{0:T(256)S(1)}, s32[256]{0:T(256)}, u32[]{:S(2)}) %copy-start.3) | copy-done | bytes 1048
  0.7 0.0 copy-start
  0.7 1.0 %copy-done = bf16[512,512]{1,0:T(8,128)(2,1)S(1)} copy-done((bf16[512,512]{1,0:T(8,128)(2,1)S(1)}, bf16[512,512]{1,0:T(8,128)(2,1)}, u32[]{:S(2)}) %copy-start) | copy-done | bytes 524312
  1.7 0.0 copy-start.1
  1.7 1.0 %copy-done.1 = bf16[512,512]{1,0:T(8,128)(2,1)S(1)} copy-done((bf16[512,512]{1,0:T(8,128)(2,1)S(1)}, bf16[512,512]{1,0:T(8,128)(2,1)}, u32[]{:S(2)}) %copy-start.1) | copy-done | bytes 524312
  2.8 0.0 copy-start.2
  2.8 1.0 %copy-done.2 = bf16[512,512]{1,0:T(8,128)(2,1)S(1)} copy-done((bf16[512,512]{1,0:T(8,128)(2,1)S(1)}, bf16[512,512]{1,0:T(8,128)(2,1)}, u32[]{:S(2)}) %copy-start.2) | copy-done | bytes 524312
  3.8 51.5 %shard_map.46 = bf16[512,512]{1,0:T(8,128)(2,1)S(1)} custom-call(bf16[512,512]{1,0:T(8,128)(2,1)S(1)} %copy-done, bf16[512,512]{1,0:T(8,128)(2,1)S(1)} %copy-done.1, bf16[512,512]{1,0:T(8,128)(2,1)S(1)} %copy-done.2, s32[1,256]{1,0:T(1,128)S(1)} %bitcast.1), custom_call_target="tpu_custom_call" | custom-call | tf_op jit(solution)/shard_map/pallas_call | solution.py:362
  55.3 0.8 %copy.6 = bf16[512,512]{1,0:T(8,128)(2,1)} copy(bf16[512,512]{1,0:T(8,128)(2,1)S(1)} %shard_map.46) | data formatting | bytes 1048576
Async XLA Ops:
  0.0 0.7 %copy-start.3 = (s32[256]{0:T(256)S(1)}, s32[256]{0:T(256)}, u32[]{:S(2)}) copy-start(s32[256]{0:T(256)} %param.7) | copy-start | bytes 3076
  0.7 1.0 %copy-start = (bf16[512,512]{1,0:T(8,128)(2,1)S(1)}, bf16[512,512]{1,0:T(8,128)(2,1)}, u32[]{:S(2)}) copy-start(bf16[512,512]{1,0:T(8,128)(2,1)} %q_ref.1) | copy-start | bytes 1572868
  1.7 1.0 %copy-start.1 = (bf16[512,512]{1,0:T(8,128)(2,1)S(1)}, bf16[512,512]{1,0:T(8,128)(2,1)}, u32[]{:S(2)}) copy-start(bf16[512,512]{1,0:T(8,128)(2,1)} %k_ref.1) | copy-start | bytes 1572868
  2.8 1.0 %copy-start.2 = (bf16[512,512]{1,0:T(8,128)(2,1)S(1)}, bf16[512,512]{1,0:T(8,128)(2,1)}, u32[]{:S(2)}) copy-start(bf16[512,512]{1,0:T(8,128)(2,1)} %v_ref.1) | copy-start | bytes 1572868

commit v2 on v1

--- a/solution.py
+++ b/solution.py
@@ -138,73 +138,92 @@
     return dot(a_high, b_high, dims) + (dot(a_high, b_low, dims) + dot(a_low, b_high, dims))
 
 
+def dot1(a, b, dims=NN):
+    return dot(a.astype(BF16), b.astype(BF16), dims)
+
+
 def fused(
-    n_seq,
     n_sub,
+    q_hbm,
+    k_hbm,
+    v_hbm,
+    len_ref,
+    out_ref,
     q_ref,
     k_ref,
     v_ref,
-    len_ref,
-    out_ref,
     part,
+    part_sib,
+    part_out,
     part_in,
     land,
     numer,
+    numer_sib,
+    numer_out,
     numer_in,
     stats,
+    stats_sib,
+    stats_out,
     stats_in,
     mix,
     weights,
+    load_sem,
     send_sem,
     recv_sem,
 ):
-    n = n_seq * n_sub
-    rows, width = q_ref.shape
-    block = width // n
-    per = HD // block
+    rows = q_ref.shape[0]
+    half = HD // 2
     pairs = H // 2
     scaling = 1.0 / math.sqrt(HD)
     me = lax.axis_index("seq") * n_sub + lax.axis_index("sub")
+    core = lax.rem(me, 2)
+    chip = lax.div(me, 2)
+    other = 1 - core
 
     def place(p):
         return {"seq": lax.div(p, n_sub), "sub": lax.rem(p, n_sub)}
 
-    def peer(step):
-        return lax.rem(me + step, n)
-
-    def remote(phase, p, source, target):
+    def copy(phase, sent, landed, p, source, target):
         return pltpu.make_async_remote_copy(
             src_ref=source,
             dst_ref=target,
-            send_sem=send_sem.at[phase, p],
-            recv_sem=recv_sem.at[phase, me],
+            send_sem=send_sem.at[phase, sent],
+            recv_sem=recv_sem.at[phase, landed],
             device_id=place(p),
             device_id_type=pl.DeviceIdType.MESH,
         )
 
-    def arrival(phase, p, target):
-        pltpu.make_async_remote_copy(
-            src_ref=target,
-            dst_ref=target,
-            send_sem=send_sem.at[phase, p],
-            recv_sem=recv_sem.at[phase, p],
-            device_id=place(p),
-            device_id_type=pl.DeviceIdType.MESH,
-        ).wait_recv()
-
-    def each_peer(act):
+    def to_sibling(phase, slot, source, target):
+        return copy(phase, slot, slot, 2 * chip + other, source, target)
+
+    def to_chip(phase, c, source, target):
+        return copy(phase, c, chip, 2 * c + core, source, target)
+
+    def arrival(phase, slot, target):
+        copy(phase, slot, slot, 2 * chip + other, target, target).wait_recv()
+
+    def each_chip(act, first=1):
         def body(step, carry):
-            act(peer(step))
+            act(lax.rem(chip + step, H))
             return carry
 
-        lax.fori_loop(1, n, body, 0)
-
+        lax.fori_loop(first, H, body, 0)
+
+    loads = [
+        pltpu.make_async_copy(source, target, load_sem.at[i])
+        for i, (source, target) in enumerate(((q_hbm, q_ref), (k_hbm, k_ref), (v_hbm, v_ref)))
+    ]
+    for load in loads:
+        load.start()
     barrier = pltpu.get_barrier_semaphore()
-    each_peer(
-        lambda p: pl.semaphore_signal(
+
+    def greet(p):
+        pl.semaphore_signal(
             barrier, inc=1, device_id=place(p), device_id_type=pl.DeviceIdType.MESH
         )
-    )
+
+    greet(2 * chip + other)
+    each_chip(lambda c: greet(2 * c + core))
 
     lengths = len_ref[...].astype(F32)
     upto = (
@@ -222,33 +241,35 @@
     member = ((positions >= begins) & (positions < ends)).astype(F32).astype(BF16)
     inverse_lengths = 1.0 / lengths
     for which, ref in enumerate((q_ref, k_ref)):
+        loads[which].wait()
         means = (dot(ref[...], member, TN) * inverse_lengths).astype(BF16)
-        for p in range(n):
-            part[p, which * block : (which + 1) * block, :] = means[p * block : (p + 1) * block]
-
-    pl.semaphore_wait(barrier, n - 1)
-    each_peer(lambda p: remote(0, p, part.at[p], part_in.at[me]).start())
+        for c in range(H):
+            part[which, c] = means[c * HD : (c + 1) * HD]
+
+    pl.semaphore_wait(barrier, H)
+    each_chip(lambda c: to_sibling(0, c, part.at[other, c], part_sib.at[c]).start())
+    to_sibling(0, chip, part.at[other, chip], part_sib.at[chip]).start()
+
+    def pass_part(c):
+        arrival(0, c, part_sib.at[c])
+        part_out[c] = (part[core, c].astype(F32) + part_sib[c].astype(F32)).astype(BF16)
+        to_chip(1, c, part_out.at[c], part_in.at[chip]).start()
+
+    each_chip(pass_part)
+    arrival(0, chip, part_sib.at[chip])
 
     def add_part(step, total):
-        p = peer(step)
-        arrival(0, p, part_in.at[p])
-        return total + part_in[p].astype(F32)
-
-    total = lax.fori_loop(1, n, add_part, part[me].astype(F32))
-    land[me] = total.astype(BF16)
-    each_peer(lambda p: remote(1, p, land.at[me], land.at[me]).start())
-
-    first = lax.div(me, per) * per
-    for i in range(per):
-        p = first + i
-
-        @pl.when(p != me)
-        def _():
-            arrival(1, p, land.at[p])
-
-    q_head = jnp.concatenate([land[first + i, :block] for i in range(per)], axis=0)
-    k_head = jnp.concatenate([land[first + i, block:] for i in range(per)], axis=0)
-    scores = dot(q_head, k_head, TN) * scaling
+        c = lax.rem(chip + step, H)
+        arrival(1, c, part_in.at[c])
+        return total + part_in[c].astype(F32)
+
+    total = part[core, chip].astype(F32) + part_sib[chip].astype(F32)
+    land[core, chip] = lax.fori_loop(1, H, add_part, total).astype(BF16)
+    to_sibling(3, chip, land.at[core, chip], land.at[core, chip]).start()
+    each_chip(lambda c: to_chip(2, c, land.at[core, chip], land.at[core, chip]).start())
+
+    arrival(3, chip, land.at[other, chip])
+    scores = dot(land[0, chip], land[1, chip], TN) * scaling
     exponentials = jnp.exp(scores - jnp.max(scores, axis=1, keepdims=True))
     kernel_two = exponentials / jnp.sum(exponentials, axis=1, keepdims=True)
     absval = jnp.abs(kernel_two)
@@ -258,32 +279,30 @@
     identity = (
         lax.broadcasted_iota(jnp.int32, (M, M), 0) == lax.broadcasted_iota(jnp.int32, (M, M), 1)
     ).astype(F32)
-    for sweep in range(ITERS):
-        product = dot3(kernel_two, inverse)
-        nested = dot3(product, 7.0 * identity - product)
-        nested = dot3(product, 15.0 * identity - nested)
-        inverse = 0.25 * dot3(inverse, 13.0 * identity - nested)
-
-    def other_arrival(p):
-        @pl.when(lax.div(p, per) != lax.div(me, per))
-        def _():
-            arrival(1, p, land.at[p])
-
-    each_peer(other_arrival)
+
+    def sweep(inverse, times):
+        product = times(kernel_two, inverse)
+        nested = times(product, 7.0 * identity - product)
+        nested = times(product, 15.0 * identity - nested)
+        return 0.25 * times(inverse, 13.0 * identity - nested)
+
+    def pass_land(c):
+        arrival(2, c, land.at[core, c])
+        to_sibling(3, c, land.at[core, c], land.at[core, c]).start()
+
+    each_chip(pass_land)
+    each_chip(lambda c: arrival(3, c, land.at[other, c]))
 
     row = lax.broadcasted_iota(jnp.int32, (2 * HD, M), 0)
 
-    def pair_operand(g, offset):
-        both = jnp.concatenate(
-            [land[p, offset : offset + block] for p in range(2 * g * per, 2 * (g + 1) * per)],
-            axis=0,
-        )
+    def pair_operand(g, which):
+        both = jnp.concatenate([land[which, 2 * g], land[which, 2 * g + 1]], axis=0)
         zero = jnp.zeros_like(both)
         return jnp.concatenate(
             [jnp.where(row < HD, both, zero), jnp.where(row < HD, zero, both)], axis=1
         )
 
-    stats[...] = jnp.zeros_like(stats)
+    loads[2].wait()
     for g in range(pairs):
         lanes = slice(g * 2 * HD, (g + 1) * 2 * HD)
         scores = dot(k_ref[:, lanes], pair_operand(g, 0)) * scaling
@@ -294,91 +313,138 @@
         for side in range(2):
             head = 2 * g + side
             columns = slice(side * M, (side + 1) * M)
-            stats[head, 0:1, :] = top[:, columns]
-            stats[head, 1:2, :] = sums[:, columns]
-            for i in range(per):
-                begin = side * HD + i * block
-                numer[head * per + i] = both[begin : begin + block, columns].astype(BF16)
-
-    def send_numer(p):
-        remote(2, p, numer.at[p], numer_in.at[me]).start()
-        remote(3, p, stats.at[lax.div(p, per)], stats_in.at[me]).start()
-
-    each_peer(send_numer)
-    numer_in[me] = numer[me]
-    stats_in[me] = stats[lax.div(me, per)]
-
+            stats[head] = pack_stats(top[:, columns], sums[:, columns])
+            for c in range(2):
+                begin = side * HD + c * half
+                numer[c, head] = both[begin : begin + half, columns].astype(BF16)
+            to_sibling(4, head, numer.at[other, head], numer_sib.at[head]).start()
+            to_sibling(5, head, stats.at[head], stats_sib.at[head]).start()
+
+    def merge(c):
+        arrival(4, c, numer_sib.at[c])
+        arrival(5, c, stats_sib.at[c])
+        a_top, a_sum = unpack_stats(stats[c])
+        b_top, b_sum = unpack_stats(stats_sib[c])
+        top = jnp.maximum(a_top, b_top)
+        a, b = jnp.exp(a_top - top), jnp.exp(b_top - top)
+        values = a * numer[core, c].astype(F32) + b * numer_sib[c].astype(F32)
+        return values.astype(BF16), pack_stats(top, a * a_sum + b * b_sum)
+
+    def pass_numer(c):
+        numer_out[c], stats_out[c] = merge(c)
+        to_chip(6, c, numer_out.at[c], numer_in.at[chip]).start()
+        to_chip(7, c, stats_out.at[c], stats_in.at[chip]).start()
+
+    each_chip(pass_numer)
+    numer_in[chip], stats_in[chip] = merge(chip)
+
+    inverse = sweep(inverse, dot1)
+    inverse = sweep(inverse, dot1)
+    inverse = sweep(inverse, dot3)
     for g in range(pairs):
         lanes = slice(g * 2 * HD, (g + 1) * 2 * HD)
-        scores = dot(q_ref[:, lanes], pair_operand(g, block)) * scaling
+        scores = dot(q_ref[:, lanes], pair_operand(g, 1)) * scaling
         for side in range(2):
             mine = scores[:, side * M : (side + 1) * M]
             weights[2 * g + side] = jnp.exp(mine - jnp.max(mine, axis=1, keepdims=True)).astype(BF16)
 
-    def numer_arrival(p):
-        arrival(2, p, numer_in.at[p])
-        arrival(3, p, stats_in.at[p])
-
-    each_peer(numer_arrival)
-    tops = [stats_in[p, 0:1, :] for p in range(n)]
-    top = functools.reduce(jnp.maximum, tops)
+    def numer_arrival(c):
+        arrival(6, c, numer_in.at[c])
+        arrival(7, c, stats_in.at[c])
+
+    each_chip(numer_arrival)
+    parts = [unpack_stats(stats_in[c]) for c in range(H)]
+    top = functools.reduce(jnp.maximum, [part_top for part_top, _ in parts])
     total = jnp.zeros((1, M), F32)
-    land_values = jnp.zeros((block, M), F32)
-    for p in range(n):
-        factor = jnp.exp(tops[p] - top)
-        total += factor * stats_in[p, 1:2, :]
-        land_values += factor * numer_in[p].astype(F32)
-    mix[me] = dot3(land_values / total, inverse, NT).astype(BF16)
-    each_peer(lambda p: remote(4, p, mix.at[me], mix.at[me]).start())
-    each_peer(lambda p: arrival(4, p, mix.at[p]))
+    land_values = jnp.zeros((half, M), F32)
+    for c, (part_top, part_sum) in enumerate(parts):
+        factor = jnp.exp(part_top - top)
+        total += factor * part_sum
+        land_values += factor * numer_in[c].astype(F32)
+    mix[core, chip] = dot3(land_values / total, inverse, NT).astype(BF16)
+    each_chip(lambda c: to_chip(8, c, mix.at[core, chip], mix.at[core, chip]).start())
+    to_sibling(9, chip, mix.at[core, chip], mix.at[core, chip]).start()
+
+    def pass_mix(c):
+        arrival(8, c, mix.at[core, c])
+        to_sibling(9, c, mix.at[core, c], mix.at[core, c]).start()
+
+    each_chip(pass_mix)
+    each_chip(lambda c: arrival(9, c, mix.at[other, c]), 0)
 
     ones = jnp.ones((HD, M), BF16)
     low = lax.broadcasted_iota(jnp.int32, (rows, 2 * HD), 1) < HD
     for g in range(pairs):
         mixed = [
-            jnp.concatenate([mix[(2 * g + side) * per + i] for i in range(per)], axis=0)
-            for side in range(2)
+            jnp.concatenate([mix[c, 2 * g + side] for c in range(2)], axis=0) for side in range(2)
         ]
         left = dot(weights[2 * g], jnp.concatenate([mixed[0], ones], axis=0), NT)
         right = dot(weights[2 * g + 1], jnp.concatenate([ones, mixed[1]], axis=0), NT)
         sums = pltpu.roll(jnp.where(low, right, left), HD, 1)
         out_ref[:, g * 2 * HD : (g + 1) * 2 * HD] = (jnp.where(low, left, right) / sums).astype(BF16)
 
-    def drain(p):
-        remote(0, p, part.at[p], part_in.at[me]).wait_send()
-        remote(1, p, land.at[me], land.at[me]).wait_send()
-        remote(2, p, numer.at[p], numer_in.at[me]).wait_send()
-        remote(3, p, stats.at[lax.div(p, per)], stats_in.at[me]).wait_send()
-        remote(4, p, mix.at[me], mix.at[me]).wait_send()
-
-    each_peer(drain)
-
-
-def fused_shards(n_seq, n_sub, queries, keys, values, seg_lengths):
-    n = n_seq * n_sub
+    def drain_chips(c):
+        to_chip(1, c, part_out.at[c], part_in.at[chip]).wait_send()
+        to_chip(2, c, land.at[core, chip], land.at[core, chip]).wait_send()
+        to_chip(6, c, numer_out.at[c], numer_in.at[chip]).wait_send()
+        to_chip(7, c, stats_out.at[c], stats_in.at[chip]).wait_send()
+        to_chip(8, c, mix.at[core, chip], mix.at[core, chip]).wait_send()
+
+    def drain_sibling(c):
+        to_sibling(0, c, part.at[other, c], part_sib.at[c]).wait_send()
+        to_sibling(3, c, land.at[core, c], land.at[core, c]).wait_send()
+        to_sibling(4, c, numer.at[other, c], numer_sib.at[c]).wait_send()
+        to_sibling(5, c, stats.at[c], stats_sib.at[c]).wait_send()
+        to_sibling(9, c, mix.at[core, c], mix.at[core, c]).wait_send()
+
+    each_chip(drain_chips)
+    each_chip(drain_sibling, 0)
+
+
+def pack_stats(top, total):
+    halves = [x[:, i * M // 2 : (i + 1) * M // 2] for x in (top, total) for i in range(2)]
+    return jnp.concatenate(halves + halves, axis=0)
+
+
+def unpack_stats(tile):
+    return (
+        jnp.concatenate([tile[0:1], tile[1:2]], axis=1),
+        jnp.concatenate([tile[2:3], tile[3:4]], axis=1),
+    )
+
+
+def fused_shards(n_sub, queries, keys, values, seg_lengths):
     rows, width = queries.shape
-    block = width // n
     vmem = pl.BlockSpec(memory_space=pltpu.VMEM)
+    hbm = pl.BlockSpec(memory_space=pl.ANY)
     return pl.pallas_call(
-        functools.partial(fused, n_seq, n_sub),
+        functools.partial(fused, n_sub),
         out_shape=jax.ShapeDtypeStruct((rows, width), BF16),
-        in_specs=[vmem] * 4,
+        in_specs=[hbm, hbm, hbm, vmem],
         out_specs=vmem,
-        scratch_shapes=[
-            pltpu.VMEM((n, 2 * block, M), BF16),
-            pltpu.VMEM((n, 2 * block, M), BF16),
-            pltpu.VMEM((n, 2 * block, M), BF16),
-            pltpu.VMEM((n, block, M), BF16),
-            pltpu.VMEM((n, block, M), BF16),
-            pltpu.VMEM((H, 8, M), F32),
-            pltpu.VMEM((n, 8, M), F32),
-            pltpu.VMEM((n, block, M), BF16),
+        scratch_shapes=[pltpu.VMEM((rows, width), BF16)] * 3
+        + [
+            pltpu.VMEM((2, H, HD, M), BF16),
+            pltpu.VMEM((H, HD, M), BF16),
+            pltpu.VMEM((H, HD, M), BF16),
+            pltpu.VMEM((H, HD, M), BF16),
+            pltpu.VMEM((2, H, HD, M), BF16),
+            pltpu.VMEM((2, H, HD // 2, M), BF16),
+            pltpu.VMEM((H, HD // 2, M), BF16),
+            pltpu.VMEM((H, HD // 2, M), BF16),
+            pltpu.VMEM((H, HD // 2, M), BF16),
+            pltpu.VMEM((H, 8, M // 2), F32),
+            pltpu.VMEM((H, 8, M // 2), F32),
+            pltpu.VMEM((H, 8, M // 2), F32),
+            pltpu.VMEM((H, 8, M // 2), F32),
+            pltpu.VMEM((2, H, HD // 2, M), BF16),
             pltpu.VMEM((H, rows, M), BF16),
-            pltpu.SemaphoreType.DMA((5, n)),
-            pltpu.SemaphoreType.DMA((5, n)),
+            pltpu.SemaphoreType.DMA((3,)),
+            pltpu.SemaphoreType.DMA((10, H)),
+            pltpu.SemaphoreType.DMA((10, H)),
         ],
         compiler_params=pltpu.CompilerParams(
-            collective_id=0, has_side_effects=True, vmem_limit_bytes=48 * 2**20
+            collective_id=0, has_side_effects=True, vmem_limit_bytes=60 * 2**20
         ),
     )(queries, keys, values, seg_lengths.reshape(1, M))
 
@@ -391,10 +457,9 @@
         P("doc"),
     )
     n_seq, n_sub = mesh.shape["seq"], mesh.shape["sub"]
-    block = H * HD // (n_seq * n_sub)
-    whole_tiles = block % 16 == 0 and HD % block == 0 and block * n_seq * n_sub == H * HD
+    chip_per_head = n_seq * n_sub == 2 * H and n_sub % 2 == 0
     return jax.shard_map(
-        functools.partial(fused_shards, n_seq, n_sub) if whole_tiles else shards,
+        functools.partial(fused_shards, n_sub) if chip_per_head else shards,
         mesh=mesh,
         in_specs=placed,
         out_specs=P(("doc", "seq", "sub"), None),

time: 56.7 us -> 42.7 us (0.75)
  Pallas kernels: 51.5 us -> 40.6 us
  local copies, waits for them, and re-layouts: 4.6 us -> 1.87 us
    pallas_call x1, Pallas kernels: 51.5 us -> 40.6 us  [fused_shards(): pl.pallas_call(functools.partial(fused, n_sub), out_shape=jax.ShapeDtypeS...]
    unnamed x9 -> x1, local copies, waits for them, and re-layouts: 4.6 us -> 1.87 us
where the time goes in v2:
time: 42.7 us; the launch traced here: 42.5 us
  Pallas kernels  40.6 us (95%)
  local copies, waits for them, and re-layouts  1.87 us (4%)
    pallas_call x1, Pallas kernels, fused_shards(): pl.pallas_call(functools.partial(fused, n_sub), out_shape=jax.ShapeDtypeS...  40.6 us
    unnamed x1, local copies, waits for them, and re-layouts  1.87 us

profile of v2, /device:TPU:1, one launch (start us, length us, event | category | flops | bytes accessed | tf_op | source)
XLA Modules:
  0.0 42.5 jit_solution(13076186091056116317)
XLA Ops:
  0.0 40.6 %shard_map.46 = bf16[512,512]{1,0:T(8,128)(2,1)} custom-call(bf16[512,512]{1,0:T(8,128)(2,1)} %q_hbm.1, bf16[512,512]{1,0:T(8,128)(2,1)} %k_hbm.1, bf16[512,512]{1,0:T(8,128)(2,1)} %v_hbm.1, s32[1,256]{1,0:T(1,128)} %bitcast.1), custom_call_target="tpu_custom_call" | custom-call | tf_op jit(solution)/shard_map/pallas_call | solution.py:420
  40.6 1.9 %copy.6 = bf16[512,512]{1,0:T(8,128)(2,1)} copy(bf16[512,512]{1,0:T(8,128)(2,1)} %shard_map.46) | data formatting | bytes 1048576

commit v3 on v2

--- a/solution.py
+++ b/solution.py
@@ -240,63 +240,79 @@
     positions = (me * rows + lax.broadcasted_iota(jnp.int32, (rows, M), 0)).astype(F32)
     member = ((positions >= begins) & (positions < ends)).astype(F32).astype(BF16)
     inverse_lengths = 1.0 / lengths
-    for which, ref in enumerate((q_ref, k_ref)):
+    def means_of(which, ref):
         loads[which].wait()
         means = (dot(ref[...], member, TN) * inverse_lengths).astype(BF16)
         for c in range(H):
-            part[which, c] = means[c * HD : (c + 1) * HD]
-
+            for side in range(2):
+                begin = c * HD + side * half
+                part[which, side, c] = means[begin : begin + half]
+
+    def send_parts(which):
+        each_chip(
+            lambda c: to_sibling(
+                10 * which, c, part.at[which, other, c], part_sib.at[which, c]
+            ).start()
+        )
+        to_sibling(
+            10 * which, chip, part.at[which, other, chip], part_sib.at[which, chip]
+        ).start()
+
+    def pass_parts(which):
+        def pass_part(c):
+            arrival(10 * which, c, part_sib.at[which, c])
+            both = part[which, core, c].astype(F32) + part_sib[which, c].astype(F32)
+            part_out[which, c] = both.astype(BF16)
+            to_chip(
+                10 * which + 1, c, part_out.at[which, c], part_in.at[which, chip]
+            ).start()
+
+        each_chip(pass_part)
+        arrival(10 * which, chip, part_sib.at[which, chip])
+
+    def add_parts(which):
+        def add_part(step, total):
+            c = lax.rem(chip + step, H)
+            arrival(10 * which + 1, c, part_in.at[which, c])
+            return total + part_in[which, c].astype(F32)
+
+        total = part[which, core, chip].astype(F32) + part_sib[which, chip].astype(F32)
+        land[which, core, chip] = lax.fori_loop(1, H, add_part, total).astype(BF16)
+        mine = land.at[which, core, chip]
+        each_chip(lambda c: to_chip(10 * which + 2, c, mine, mine).start())
+        to_sibling(10 * which + 3, chip, mine, mine).start()
+
+    def pass_lands(which):
+        def pass_land(c):
+            arrival(10 * which + 2, c, land.at[which, core, c])
+            to_sibling(
+                10 * which + 3, c, land.at[which, core, c], land.at[which, core, c]
+            ).start()
+
+        each_chip(pass_land)
+
+    def await_lands(which):
+        each_chip(lambda c: arrival(10 * which + 3, c, land.at[which, other, c]))
+
+    means_of(0, q_ref)
     pl.semaphore_wait(barrier, H)
-    each_chip(lambda c: to_sibling(0, c, part.at[other, c], part_sib.at[c]).start())
-    to_sibling(0, chip, part.at[other, chip], part_sib.at[chip]).start()
-
-    def pass_part(c):
-        arrival(0, c, part_sib.at[c])
-        part_out[c] = (part[core, c].astype(F32) + part_sib[c].astype(F32)).astype(BF16)
-        to_chip(1, c, part_out.at[c], part_in.at[chip]).start()
-
-    each_chip(pass_part)
-    arrival(0, chip, part_sib.at[chip])
-
-    def add_part(step, total):
-        c = lax.rem(chip + step, H)
-        arrival(1, c, part_in.at[c])
-        return total + part_in[c].astype(F32)
-
-    total = part[core, chip].astype(F32) + part_sib[chip].astype(F32)
-    land[core, chip] = lax.fori_loop(1, H, add_part, total).astype(BF16)
-    to_sibling(3, chip, land.at[core, chip], land.at[core, chip]).start()
-    each_chip(lambda c: to_chip(2, c, land.at[core, chip], land.at[core, chip]).start())
-
-    arrival(3, chip, land.at[other, chip])
-    scores = dot(land[0, chip], land[1, chip], TN) * scaling
-    exponentials = jnp.exp(scores - jnp.max(scores, axis=1, keepdims=True))
-    kernel_two = exponentials / jnp.sum(exponentials, axis=1, keepdims=True)
-    absval = jnp.abs(kernel_two)
-    row_most = jnp.max(jnp.sum(absval, axis=1, keepdims=True), axis=0, keepdims=True)
-    col_most = jnp.max(jnp.sum(absval, axis=0, keepdims=True), axis=1, keepdims=True)
-    inverse = kernel_two.T / (row_most * col_most)
-    identity = (
-        lax.broadcasted_iota(jnp.int32, (M, M), 0) == lax.broadcasted_iota(jnp.int32, (M, M), 1)
-    ).astype(F32)
-
-    def sweep(inverse, times):
-        product = times(kernel_two, inverse)
-        nested = times(product, 7.0 * identity - product)
-        nested = times(product, 15.0 * identity - nested)
-        return 0.25 * times(inverse, 13.0 * identity - nested)
-
-    def pass_land(c):
-        arrival(2, c, land.at[core, c])
-        to_sibling(3, c, land.at[core, c], land.at[core, c]).start()
-
-    each_chip(pass_land)
-    each_chip(lambda c: arrival(3, c, land.at[other, c]))
+    send_parts(0)
+    means_of(1, k_ref)
+    pass_parts(0)
+    send_parts(1)
+    add_parts(0)
+    pass_parts(1)
+    pass_lands(0)
+    arrival(3, chip, land.at[0, other, chip])
+    await_lands(0)
+
+    def head_land(which, c):
+        return jnp.concatenate([land[which, side, c] for side in range(2)], axis=0)
 
     row = lax.broadcasted_iota(jnp.int32, (2 * HD, M), 0)
 
     def pair_operand(g, which):
-        both = jnp.concatenate([land[which, 2 * g], land[which, 2 * g + 1]], axis=0)
+        both = jnp.concatenate([head_land(which, 2 * g), head_land(which, 2 * g + 1)], axis=0)
         zero = jnp.zeros_like(both)
         return jnp.concatenate(
             [jnp.where(row < HD, both, zero), jnp.where(row < HD, zero, both)], axis=1
@@ -338,15 +354,29 @@
     each_chip(pass_numer)
     numer_in[chip], stats_in[chip] = merge(chip)
 
+    add_parts(1)
+    arrival(13, chip, land.at[1, other, chip])
+    scores = dot(head_land(0, chip), head_land(1, chip), TN) * scaling
+    exponentials = jnp.exp(scores - jnp.max(scores, axis=1, keepdims=True))
+    kernel_two = exponentials / jnp.sum(exponentials, axis=1, keepdims=True)
+    absval = jnp.abs(kernel_two)
+    row_most = jnp.max(jnp.sum(absval, axis=1, keepdims=True), axis=0, keepdims=True)
+    col_most = jnp.max(jnp.sum(absval, axis=0, keepdims=True), axis=1, keepdims=True)
+    inverse = kernel_two.T / (row_most * col_most)
+    identity = (
+        lax.broadcasted_iota(jnp.int32, (M, M), 0) == lax.broadcasted_iota(jnp.int32, (M, M), 1)
+    ).astype(F32)
+
+    def sweep(inverse, times):
+        product = times(kernel_two, inverse)
+        nested = times(product, 7.0 * identity - product)
+        nested = times(product, 15.0 * identity - nested)
+        return 0.25 * times(inverse, 13.0 * identity - nested)
+
     inverse = sweep(inverse, dot1)
     inverse = sweep(inverse, dot1)
     inverse = sweep(inverse, dot3)
-    for g in range(pairs):
-        lanes = slice(g * 2 * HD, (g + 1) * 2 * HD)
-        scores = dot(q_ref[:, lanes], pair_operand(g, 1)) * scaling
-        for side in range(2):
-            mine = scores[:, side * M : (side + 1) * M]
-            weights[2 * g + side] = jnp.exp(mine - jnp.max(mine, axis=1, keepdims=True)).astype(BF16)
+    pass_lands(1)
 
     def numer_arrival(c):
         arrival(6, c, numer_in.at[c])
@@ -365,6 +395,14 @@
     each_chip(lambda c: to_chip(8, c, mix.at[core, chip], mix.at[core, chip]).start())
     to_sibling(9, chip, mix.at[core, chip], mix.at[core, chip]).start()
 
+    await_lands(1)
+    for g in range(pairs):
+        lanes = slice(g * 2 * HD, (g + 1) * 2 * HD)
+        scores = dot(q_ref[:, lanes], pair_operand(g, 1)) * scaling
+        for side in range(2):
+            mine = scores[:, side * M : (side + 1) * M]
+            weights[2 * g + side] = jnp.exp(mine - jnp.max(mine, axis=1, keepdims=True)).astype(BF16)
+
     def pass_mix(c):
         arrival(8, c, mix.at[core, c])
         to_sibling(9, c, mix.at[core, c], mix.at[core, c]).start()
@@ -384,15 +422,23 @@
         out_ref[:, g * 2 * HD : (g + 1) * 2 * HD] = (jnp.where(low, left, right) / sums).astype(BF16)
 
     def drain_chips(c):
-        to_chip(1, c, part_out.at[c], part_in.at[chip]).wait_send()
-        to_chip(2, c, land.at[core, chip], land.at[core, chip]).wait_send()
+        for which in range(2):
+            mine = land.at[which, core, chip]
+            to_chip(
+                10 * which + 1, c, part_out.at[which, c], part_in.at[which, chip]
+            ).wait_send()
+            to_chip(10 * which + 2, c, mine, mine).wait_send()
         to_chip(6, c, numer_out.at[c], numer_in.at[chip]).wait_send()
         to_chip(7, c, stats_out.at[c], stats_in.at[chip]).wait_send()
         to_chip(8, c, mix.at[core, chip], mix.at[core, chip]).wait_send()
 
     def drain_sibling(c):
-        to_sibling(0, c, part.at[other, c], part_sib.at[c]).wait_send()
-        to_sibling(3, c, land.at[core, c], land.at[core, c]).wait_send()
+        for which in range(2):
+            block = land.at[which, core, c]
+            to_sibling(
+                10 * which, c, part.at[which, other, c], part_sib.at[which, c]
+            ).wait_send()
+            to_sibling(10 * which + 3, c, block, block).wait_send()
         to_sibling(4, c, numer.at[other, c], numer_sib.at[c]).wait_send()
         to_sibling(5, c, stats.at[c], stats_sib.at[c]).wait_send()
         to_sibling(9, c, mix.at[core, c], mix.at[core, c]).wait_send()
@@ -424,11 +470,11 @@
         out_specs=vmem,
         scratch_shapes=[pltpu.VMEM((rows, width), BF16)] * 3
         + [
-            pltpu.VMEM((2, H, HD, M), BF16),
-            pltpu.VMEM((H, HD, M), BF16),
-            pltpu.VMEM((H, HD, M), BF16),
-            pltpu.VMEM((H, HD, M), BF16),
-            pltpu.VMEM((2, H, HD, M), BF16),
+            pltpu.VMEM((2, 2, H, HD // 2, M), BF16),
+            pltpu.VMEM((2, H, HD // 2, M), BF16),
+            pltpu.VMEM((2, H, HD // 2, M), BF16),
+            pltpu.VMEM((2, H, HD // 2, M), BF16),
+            pltpu.VMEM((2, 2, H, HD // 2, M), BF16),
             pltpu.VMEM((2, H, HD // 2, M), BF16),
             pltpu.VMEM((H, HD // 2, M), BF16),
             pltpu.VMEM((H, HD // 2, M), BF16),
@@ -440,8 +486,8 @@
             pltpu.VMEM((2, H, HD // 2, M), BF16),
             pltpu.VMEM((H, rows, M), BF16),
             pltpu.SemaphoreType.DMA((3,)),
-            pltpu.SemaphoreType.DMA((10, H)),
-            pltpu.SemaphoreType.DMA((10, H)),
+            pltpu.SemaphoreType.DMA((14, H)),
+            pltpu.SemaphoreType.DMA((14, H)),
         ],
         compiler_params=pltpu.CompilerParams(
             collective_id=0, has_side_effects=True, vmem_limit_bytes=60 * 2**20

time: 42.7 us -> 41.9 us (0.981)
  Pallas kernels: 40.6 us -> 39.8 us
    pallas_call x1, Pallas kernels: 40.6 us -> 39.8 us  [fused_shards(): pl.pallas_call(functools.partial(fused, n_sub), out_shape=jax.ShapeDtypeS...]
where the time goes in v3:
time: 41.9 us; the launch traced here: 41.7 us
  Pallas kernels  39.8 us (95%)
  local copies, waits for them, and re-layouts  1.87 us (4%)
    pallas_call x1, Pallas kernels, fused_shards(): pl.pallas_call(functools.partial(fused, n_sub), out_shape=jax.ShapeDtypeS...  39.8 us
    unnamed x1, local copies, waits for them, and re-layouts  1.87 us

profile of v3, /device:TPU:1, one launch (start us, length us, event | category | flops | bytes accessed | tf_op | source)
XLA Modules:
  0.0 41.7 jit_solution(8420186948238283891)
XLA Ops:
  0.0 39.8 %shard_map.46 = bf16[512,512]{1,0:T(8,128)(2,1)} custom-call(bf16[512,512]{1,0:T(8,128)(2,1)} %q_hbm.1, bf16[512,512]{1,0:T(8,128)(2,1)} %k_hbm.1, bf16[512,512]{1,0:T(8,128)(2,1)} %v_hbm.1, s32[1,256]{1,0:T(1,128)} %bitcast.1), custom_call_target="tpu_custom_call" | custom-call | tf_op jit(solution)/shard_map/pallas_call | solution.py:466
  39.8 1.9 %copy.6 = bf16[512,512]{1,0:T(8,128)(2,1)} copy(bf16[512,512]{1,0:T(8,128)(2,1)} %shard_map.46) | data formatting | bytes 1048576
